TPU v7x, 32 devices: a whole 2x2x4 slice. The times are simulated.
32 devices in a mesh: dp: 8 (over z, y), seq: 4 (over x, core).
Axes of the slice: x: 2, y: 2, z: 4, core: 2. Of those that a mesh axis runs over, the one named last changes fastest.
Arguments:
- inputs: bfloat16 [16, 1024, 1280], P('dp', 'seq'), may hold values from -6 to 6
- w_query: bfloat16 [1280, 1280], P(('dp', 'seq')), may hold values from -0.15625 to 0.15625
- w_key: bfloat16 [1280, 1280], P(('dp', 'seq')), may hold values from -0.15625 to 0.15625
- w_value: bfloat16 [1280, 1280], P(('dp', 'seq')), may hold values from -0.15625 to 0.15625
- w_out: bfloat16 [1280, 1280], P(('dp', 'seq')), may hold values from -0.625 to 0.625
- w_up: bfloat16 [1280, 1280], P(('dp', 'seq')), may hold values from -0.15625 to 0.15625
- w_down: bfloat16 [1280, 1280], P(('dp', 'seq')), may hold values from -0.3125 to 0.3125
- gain_attn: bfloat16 [1280], P(('dp', 'seq')), may hold values from 0.099609375 to 1.8984375
- gain_mlp: bfloat16 [1280], P(('dp', 'seq')), may hold values from 0.099609375 to 1.8984375
- pad_patches: int32 [16], P('dp'), may hold values from 0 to 1023, as said below
- cotangent: bfloat16 [16, 1024, 1280], P('dp', 'seq'), may hold values from -6 to 6
Outputs:
- layer_out: bfloat16 [16, 1024, 1280], P('dp', 'seq')
- grad_input: float32 [16, 1024, 1280], P('dp', 'seq')
- grad_query: float32 [1280, 1280], P(('dp', 'seq'))
- grad_key: float32 [1280, 1280], P(('dp', 'seq'))
- grad_value: float32 [1280, 1280], P(('dp', 'seq'))
- grad_outproj: float32 [1280, 1280], P(('dp', 'seq'))
- grad_upproj: float32 [1280, 1280], P(('dp', 'seq'))
- grad_downproj: float32 [1280, 1280], P(('dp', 'seq'))
- grad_gain_attn: float32 [1280], P(('dp', 'seq'))
- grad_gain_mlp: float32 [1280], P(('dp', 'seq'))
Inputs may be any that keep to these rules, and one draw needn't show every extreme that they name: `pad_patches`: in each group of 2 contexts held by one index of dp, one context has fewer than 256 padding patches. Some context has no padding and some has 1023 padding patches.
All inputs are finite; a program needn't handle non-finite values.
Results may differ from a plain program's by a relative error of at most 0.03.
Values may be sent and summed in bfloat16 or wider, within the bound.
A program may use at most 256 MiB of HBM per device.

v0:
```python
import jax
import jax.numpy as jnp
from jax import lax
from jax.sharding import PartitionSpec as P

HEADS = 16
HEAD_DIM = 80


def shifted(value, axis, steps):
    count = lax.axis_size(axis)
    initial, last = (max(0, -steps), min(count, count - steps))
    return lax.ppermute(value, axis, [(source, source + steps) for source in range(initial, last)])


def rms_scale(values):
    return lax.rsqrt(jnp.mean(values * values, axis=-1, keepdims=True) + 1e-06)


def rms_back(values, scale, gain, grad_norm):
    scaled_grad = grad_norm * gain
    grad_gain = jnp.sum(grad_norm * values * scale, axis=0)
    grad_values = scale * scaled_grad - values * (scale * scale * scale) * jnp.mean(
        scaled_grad * values, axis=-1, keepdims=True
    )
    return (grad_values, grad_gain)


def rope_tables(positions, half):
    freqs = 10000.0 ** (-jnp.arange(half, dtype=jnp.float32) / half)
    angles = positions[:, None].astype(jnp.float32) * freqs[None, :]
    return (jnp.cos(angles), jnp.sin(angles))


def rotate_pairs(tensor, cosine, sine):
    half = tensor.shape[-1] // 2
    first = tensor[..., :half]
    second = tensor[..., half:]
    cos_b = cosine[None, :, None, :]
    sin_b = sine[None, :, None, :]
    return jnp.concatenate(
        [first * cos_b - second * sin_b, first * sin_b + second * cos_b], axis=-1
    )


def rotate_back(tensor, cosine, sine):
    half = tensor.shape[-1] // 2
    first = tensor[..., :half]
    second = tensor[..., half:]
    cos_b = cosine[None, :, None, :]
    sin_b = sine[None, :, None, :]
    return jnp.concatenate(
        [first * cos_b + second * sin_b, second * cos_b - first * sin_b], axis=-1
    )


def block_weights(queries, key_block, source, positions, pad_patches, patches):
    scale_factor = queries.shape[-1] ** (-0.5)
    scores = scale_factor * jnp.einsum(
        "sqhd,skhd->shqk", queries, key_block, preferred_element_type=jnp.float32
    )
    key_pos = source * patches + jnp.arange(patches, dtype=jnp.int32)
    key_grid = key_pos[None, None, :]
    query_grid = positions[None, :, None]
    allowed = (
        (key_grid <= query_grid)
        & ((key_grid >= pad_patches[:, None, None]) | (key_grid == query_grid))
        & (source >= 0)
    )
    allowed = allowed[:, None]
    masked = jnp.where(allowed, scores, -1e30)
    peaks = jnp.max(masked, axis=-1)
    expo = jnp.exp(masked - peaks[..., None]) * allowed.astype(jnp.float32)
    return (expo, peaks)


def block_forward(queries, key_block, value_block, source, positions, pad_patches, patches):
    expo, peaks = block_weights(queries, key_block, source, positions, pad_patches, patches)
    masses = jnp.sum(expo, axis=-1)
    partials = jnp.einsum(
        "shqk,skhd->sqhd",
        expo.astype(jnp.bfloat16),
        value_block,
        preferred_element_type=jnp.float32,
    )
    return (peaks, masses, partials)


def block_backward(
    queries,
    key_block,
    value_block,
    source,
    positions,
    pad_patches,
    patches,
    summit,
    total,
    delta,
    grad_attn,
):
    expo, peaks = block_weights(queries, key_block, source, positions, pad_patches, patches)
    share = jnp.exp(peaks - summit) / total
    share_tok = jnp.swapaxes(share, 1, 2)[..., None]
    grad_part = (share_tok * grad_attn).astype(jnp.bfloat16)
    grad_vblock = jnp.einsum(
        "shqk,sqhd->skhd", expo.astype(jnp.bfloat16), grad_part, preferred_element_type=jnp.float32
    )
    grad_prob = jnp.einsum(
        "sqhd,skhd->shqk", grad_part, value_block, preferred_element_type=jnp.float32
    )
    grad_scores = (expo * (grad_prob - (share * delta)[..., None])).astype(jnp.bfloat16)
    grad_qblock = jnp.einsum(
        "shqk,skhd->sqhd", grad_scores, key_block, preferred_element_type=jnp.float32
    )
    grad_kblock = jnp.einsum(
        "shqk,sqhd->skhd", grad_scores, queries, preferred_element_type=jnp.float32
    )
    return (grad_qblock, grad_kblock, grad_vblock)


def body(
    inputs,
    w_query,
    w_key,
    w_value,
    w_out,
    w_up,
    w_down,
    gain_attn,
    gain_mlp,
    pad_patches,
    cotangent,
):
    contexts, patches, model_width = inputs.shape
    head_count = HEADS
    head_size = HEAD_DIM
    seq_count = lax.axis_size("seq")
    seq_rank = lax.axis_index("seq")
    token_rows = contexts * patches
    shape_heads = (contexts, patches, head_count, head_size)
    shape_flat = (contexts, patches, model_width)
    shards = (w_query, w_key, w_value, w_out, w_up, w_down, gain_attn, gain_mlp)
    gathered = (
        lax.all_gather(shards[0], ("dp", "seq"), axis=0, tiled=True),
        lax.all_gather(shards[1], ("dp", "seq"), axis=0, tiled=True),
        lax.all_gather(shards[2], ("dp", "seq"), axis=0, tiled=True),
        lax.all_gather(shards[3], ("dp", "seq"), axis=0, tiled=True),
        lax.all_gather(shards[4], ("dp", "seq"), axis=0, tiled=True),
        lax.all_gather(shards[5], ("dp", "seq"), axis=0, tiled=True),
        lax.all_gather(shards[6], ("dp", "seq"), axis=0, tiled=True),
        lax.all_gather(shards[7], ("dp", "seq"), axis=0, tiled=True),
    )
    full_q, full_k, full_v, full_o, full_up, full_down, full_ga, full_gm = gathered
    positions = seq_rank * patches + jnp.arange(patches, dtype=jnp.int32)
    cosine, sine = rope_tables(positions, head_size // 2)
    inputs_f = inputs.astype(jnp.float32).reshape(token_rows, model_width)
    gain_one = full_ga.astype(jnp.float32)
    scale_one = rms_scale(inputs_f)
    flat_attn = (inputs_f * scale_one * gain_one).astype(jnp.bfloat16)
    query_lin = jnp.dot(flat_attn, full_q, preferred_element_type=jnp.float32).reshape(shape_heads)
    key_lin = jnp.dot(flat_attn, full_k, preferred_element_type=jnp.float32).reshape(shape_heads)
    value_flat = jnp.dot(flat_attn, full_v, preferred_element_type=jnp.float32).astype(jnp.bfloat16)
    queries = rotate_pairs(query_lin, cosine, sine).astype(jnp.bfloat16)
    key_flat = rotate_pairs(key_lin, cosine, sine).astype(jnp.bfloat16)
    own_blocks = (key_flat.reshape(shape_flat), value_flat.reshape(shape_flat))
    kept = []
    sources = []
    current = own_blocks
    for offset in range(seq_count):
        if offset > 0:
            current = shifted((current[0], current[1]), "seq", 1)
        kept.append(current)
        sources.append(seq_rank - offset)
    stats = []
    for block_pair, source_idx in zip(kept, sources):
        stats.append(
            block_forward(
                queries,
                block_pair[0].reshape(shape_heads),
                block_pair[1].reshape(shape_heads),
                source_idx,
                positions,
                pad_patches,
                patches,
            )
        )
    peaks = jnp.stack([entry[0] for entry in stats])
    masses = jnp.stack([entry[1] for entry in stats])
    partials = jnp.stack([entry[2] for entry in stats])
    summit = jnp.max(peaks, axis=0)
    weights_blk = jnp.exp(peaks - summit[None])
    total = jnp.sum(weights_blk * masses, axis=0)
    attended = (
        jnp.sum(jnp.swapaxes(weights_blk, 2, 3)[..., None] * partials, axis=0)
        / jnp.swapaxes(total, 1, 2)[..., None]
    )
    attn_low = attended.astype(jnp.bfloat16).reshape(token_rows, model_width)
    branch = jnp.dot(attn_low, full_o, preferred_element_type=jnp.float32)
    hidden = inputs_f + branch
    gain_two = full_gm.astype(jnp.float32)
    scale_two = rms_scale(hidden)
    norm_mlp = (hidden * scale_two * gain_two).astype(jnp.bfloat16)
    upper = jnp.dot(norm_mlp, full_up, preferred_element_type=jnp.float32)
    active = jax.nn.silu(upper).astype(jnp.bfloat16)
    mlp_out = jnp.dot(active, full_down, preferred_element_type=jnp.float32)
    layer_out = (hidden + mlp_out).astype(jnp.bfloat16).reshape(shape_flat)
    back_q, back_k, back_v, back_o, back_up, back_down, back_ga, back_gm = gathered
    cot_low = cotangent.reshape(token_rows, model_width)
    cot_full = cot_low.astype(jnp.float32)
    grad_downw = jnp.dot(active.T, cot_low, preferred_element_type=jnp.float32)
    grad_active = jnp.dot(cot_low, back_down.T, preferred_element_type=jnp.float32)
    sigmoid_up = jax.nn.sigmoid(upper)
    grad_upper = (grad_active * sigmoid_up * (1.0 + upper * (1.0 - sigmoid_up))).astype(
        jnp.bfloat16
    )
    grad_upw = jnp.dot(norm_mlp.T, grad_upper, preferred_element_type=jnp.float32)
    grad_norm_mlp = jnp.dot(grad_upper, back_up.T, preferred_element_type=jnp.float32)
    grad_from_mlp, grad_gain_two = rms_back(
        hidden, scale_two, back_gm.astype(jnp.float32), grad_norm_mlp
    )
    grad_hidden = cot_full + grad_from_mlp
    hid_low = grad_hidden.astype(jnp.bfloat16)
    grad_outw = jnp.dot(attn_low.T, hid_low, preferred_element_type=jnp.float32)
    grad_attn = jnp.dot(hid_low, back_o.T, preferred_element_type=jnp.float32).astype(jnp.bfloat16)
    grad_attn_f = grad_attn.astype(jnp.float32).reshape(shape_heads)
    delta = jnp.swapaxes(jnp.sum(grad_attn_f * attended, axis=-1), 1, 2)
    grad_queries = jnp.zeros(shape_heads, jnp.float32)
    carried = (jnp.zeros(shape_flat, jnp.float32), jnp.zeros(shape_flat, jnp.float32))
    for offset in reversed(range(seq_count)):
        block_pair = kept[offset]
        part_q, part_k, part_v = block_backward(
            queries,
            block_pair[0].reshape(shape_heads),
            block_pair[1].reshape(shape_heads),
            sources[offset],
            positions,
            pad_patches,
            patches,
            summit,
            total,
            delta,
            grad_attn_f,
        )
        grad_queries = grad_queries + part_q
        carried = (carried[0] + part_k.reshape(shape_flat), carried[1] + part_v.reshape(shape_flat))
        if offset > 0:
            carried = (
                shifted(carried[0].astype(jnp.bfloat16), "seq", -1).astype(jnp.float32),
                shifted(carried[1].astype(jnp.bfloat16), "seq", -1).astype(jnp.float32),
            )
    grad_keys, grad_values = carried
    scale_factor = head_size ** (-0.5)
    grad_qlin = (
        rotate_back(grad_queries * scale_factor, cosine, sine)
        .astype(jnp.bfloat16)
        .reshape(token_rows, model_width)
    )
    grad_klin = (
        rotate_back(grad_keys.reshape(shape_heads) * scale_factor, cosine, sine)
        .astype(jnp.bfloat16)
        .reshape(token_rows, model_width)
    )
    grad_vlin = grad_values.astype(jnp.bfloat16).reshape(token_rows, model_width)
    grad_qw = jnp.dot(flat_attn.T, grad_qlin, preferred_element_type=jnp.float32)
    grad_kw = jnp.dot(flat_attn.T, grad_klin, preferred_element_type=jnp.float32)
    grad_vw = jnp.dot(flat_attn.T, grad_vlin, preferred_element_type=jnp.float32)
    grad_norm_attn = jnp.dot(grad_qlin, back_q.T, preferred_element_type=jnp.float32)
    grad_norm_attn = grad_norm_attn + jnp.dot(
        grad_klin, back_k.T, preferred_element_type=jnp.float32
    )
    grad_norm_attn = grad_norm_attn + jnp.dot(
        grad_vlin, back_v.T, preferred_element_type=jnp.float32
    )
    grad_from_attn, grad_gain_one = rms_back(
        inputs_f, scale_one, back_ga.astype(jnp.float32), grad_norm_attn
    )
    grad_input = (grad_hidden + grad_from_attn).reshape(shape_flat)
    totals = (
        lax.psum_scatter(grad_qw, ("dp", "seq"), scatter_dimension=0, tiled=True),
        lax.psum_scatter(grad_kw, ("dp", "seq"), scatter_dimension=0, tiled=True),
        lax.psum_scatter(grad_vw, ("dp", "seq"), scatter_dimension=0, tiled=True),
        lax.psum_scatter(grad_outw, ("dp", "seq"), scatter_dimension=0, tiled=True),
        lax.psum_scatter(grad_upw, ("dp", "seq"), scatter_dimension=0, tiled=True),
        lax.psum_scatter(grad_downw, ("dp", "seq"), scatter_dimension=0, tiled=True),
        lax.psum_scatter(grad_gain_one, ("dp", "seq"), scatter_dimension=0, tiled=True),
        lax.psum_scatter(grad_gain_two, ("dp", "seq"), scatter_dimension=0, tiled=True),
    )
    return (
        layer_out,
        grad_input,
        totals[0],
        totals[1],
        totals[2],
        totals[3],
        totals[4],
        totals[5],
        totals[6],
        totals[7],
    )


def solution(mesh):
    placed = (
        P("dp", "seq", None),
        P(("dp", "seq"), None),
        P(("dp", "seq"), None),
        P(("dp", "seq"), None),
        P(("dp", "seq"), None),
        P(("dp", "seq"), None),
        P(("dp", "seq"), None),
        P(("dp", "seq")),
        P(("dp", "seq")),
        P("dp"),
        P("dp", "seq", None),
    )
    return jax.shard_map(
        body,
        mesh=mesh,
        in_specs=placed,
        out_specs=(
            P("dp", "seq", None),
            P("dp", "seq", None),
            P(("dp", "seq"), None),
            P(("dp", "seq"), None),
            P(("dp", "seq"), None),
            P(("dp", "seq"), None),
            P(("dp", "seq"), None),
            P(("dp", "seq"), None),
            P(("dp", "seq")),
            P(("dp", "seq")),
        ),
        check_vma=False,
    )
```

profile of v0, /device:TPU:0, one launch (start us, length us, event | category | flops | bytes accessed | tf_op | source)
XLA Modules:
  0.0 1267.3 jit_solution(2679474405545930290)
XLA Ops:
  14.7 42.4 %all-reduce.5 = (bf16[1280]{0:T(1024)(128)(2,1)S(1)}, bf16[1280]{0:T(1024)(128)(2,1)S(1)}) all-reduce(bf16[1280]{0:T(1024)(128)(2,1)S(1)} %dynamic-update-slice, bf16[1280]{0:T(1024)(128)(2,1)S(1)} %dynamic-update-slice.1), channel_id=1, replica_groups=mesh['dp'=8,'seq'=4] {'dp','seq'}, use_global_device_ids=true, to_apply=%add | all-reduce | flops 2560 | bytes 10240
  64.4 8.5 all-gather.11.cloned.1.call-done
  81.4 52.6 %all-gather.9.cloned.1.call-done = bf16[1280,1280]{1,0:T(8,128)(2,1)} async-done(((bf16[40,1280]{1,0:T(8,128)(2,1)}), bf16[1280,1280]{1,0:T(8,128)(2,1)}) %all-gather.9.cloned.1.call-update) | async-done | bytes 3276816 | tf_op jit(solution)/shard_map/all_gather | solution.py:146
  148.6 46.4 %all-gather.7.cloned.1.call-done = bf16[1280,1280]{1,0:T(8,128)(2,1)} async-done(((bf16[40,1280]{1,0:T(8,128)(2,1)}), bf16[1280,1280]{1,0:T(8,128)(2,1)}) %all-gather.7.cloned.1.call-update) | async-done | bytes 3276816 | tf_op jit(solution)/shard_map/all_gather | solution.py:145
  223.1 7.7 convolution_bitcast_fusion.4
  246.1 7.6 convolution_bitcast_fusion.3
  262.4 11.9 collective-permute-start.5
  312.5 7.1 all-gather.15.cloned.1.call-done
  325.8 56.8 %all-gather.17.cloned.1.call-done = bf16[1280,1280]{1,0:T(8,128)(2,1)} async-done(((bf16[40,1280]{1,0:T(8,128)(2,1)}), bf16[1280,1280]{1,0:T(8,128)(2,1)}) %all-gather.17.cloned.1.call-update) | async-done | bytes 3276816 | tf_op jit(solution)/shard_map/all_gather | solution.py:150
  446.7 6.8 multiply_convert_fusion.2
  458.8 6.7 multiply_convert_fusion
  496.2 23.5 %collective-permute-done.8 = bf16[2,256,1280]{1,2,0:T(8,128)(2,1)S(1)} collective-permute-done((bf16[2,256,1280]{1,2,0:T(8,128)(2,1)S(1)}, bf16[2,256,1280]{1,2,0:T(8,128)(2,1)S(1)}, u32[]{:S(2)}, u32[]{:S(2)}) %collective-permute-start.8) | collective-permute-done | bytes 1310752 | tf_op jit(solution)/shard_map/ppermute | solution.py:13
  538.7 6.8 convolution_convert_fusion.2
  549.3 7.2 fusion.39
  559.7 11.9 collective-permute-done.9
  576.4 7.3 fusion.40
  586.9 20.4 %collective-permute-done.10 = bf16[2,256,1280]{2,1,0:T(8,128)(2,1)} collective-permute-done((bf16[2,256,1280]{2,1,0:T(8,128)(2,1)}, bf16[2,256,1280]{2,1,0:T(8,128)(2,1)}, u32[]{:S(2)}, u32[]{:S(2)}) %collective-permute-start.10) | collective-permute-done | bytes 1310752 | tf_op jit(solution)/shard_map/ppermute | solution.py:13
  612.3 7.3 fusion.41
  621.8 21.3 %collective-permute-done.11 = bf16[2,256,1280]{2,1,0:T(8,128)(2,1)} collective-permute-done((bf16[2,256,1280]{2,1,0:T(8,128)(2,1)}, bf16[2,256,1280]{2,1,0:T(8,128)(2,1)}, u32[]{:S(2)}, u32[]{:S(2)}) %collective-permute-start.11) | collective-permute-done | bytes 1310752 | tf_op jit(solution)/shard_map/ppermute | solution.py:13
  667.1 70.9 %all-reduce.4 = (f32[1280]{0:T(1024)S(1)}, f32[1280]{0:T(1024)S(1)}) all-reduce(f32[1280]{0:T(1024)S(1)} %get-tuple-element.12, f32[1280]{0:T(1024)S(1)} %copy-done.79), channel_id=8, replica_groups=mesh['dp'=8,'seq'=4] {'dp','seq'}, use_global_device_ids=true, to_apply=%region_22.23.clone | all-reduce | flops 2560 | bytes 20480
  743.9 83.7 %reduce-scatter.17.cloned.1.call-done = f32[40,1280]{1,0:T(8,128)} async-done(((f32[1280,1280]{1,0:T(8,128)}), f32[40,1280]{1,0:T(8,128)}) %reduce-scatter.17.cloned.1.call-update) | async-done | bytes 204816 | tf_op jit(solution)/shard_map/reduce_scatter | solution.py:285
  827.6 144.2 %reduce-scatter.9.cloned.1.call-done = f32[40,1280]{1,0:T(8,128)} async-done(((f32[1280,1280]{1,0:T(8,128)}), f32[40,1280]{1,0:T(8,128)}) %reduce-scatter.9.cloned.1.call-update) | async-done | bytes 204816 | tf_op jit(solution)/shard_map/reduce_scatter | solution.py:281
  971.8 144.2 %reduce-scatter.7.cloned.1.call-done = f32[40,1280]{1,0:T(8,128)} async-done(((f32[1280,1280]{1,0:T(8,128)}), f32[40,1280]{1,0:T(8,128)}) %reduce-scatter.7.cloned.1.call-update) | async-done | bytes 204816 | tf_op jit(solution)/shard_map/reduce_scatter | solution.py:280
  1116.0 144.0 %reduce-scatter.11.cloned.1.call-done = f32[40,1280]{1,0:T(8,128)} async-done(((f32[1280,1280]{1,0:T(8,128)}), f32[40,1280]{1,0:T(8,128)}) %reduce-scatter.11.cloned.1.call-update) | async-done | bytes 204816 | tf_op jit(solution)/shard_map/reduce_scatter | solution.py:282
  (330 shorter events, 304.2 us)
Async XLA Ops:
  7.2 65.7 %all-gather.11.cloned.1.call-start = ((), (), s32[]{:S(2)}) async-start(), calls=%async_computation.8 | async-start | bytes 3379200 | tf_op jit(solution)/shard_map/all_gather | solution.py:147
  7.9 126.0 %all-gather.9.cloned.1.call-start = ((), (), s32[]{:S(2)}) async-start(), calls=%async_computation.7 | async-start | bytes 3379200 | tf_op jit(solution)/shard_map/all_gather | solution.py:146
  8.7 186.3 %all-gather.7.cloned.1.call-start = ((), (), s32[]{:S(2)}) async-start(), calls=%async_computation.6 | async-start | bytes 3379200 | tf_op jit(solution)/shard_map/all_gather | solution.py:145
  9.4 297.2 %all-gather.13.cloned.1.call-start = ((), (), s32[]{:S(2)}) async-start(), calls=%async_computation.9 | async-start | bytes 3379200 | tf_op jit(solution)/shard_map/all_gather | solution.py:148
  10.0 309.7 %all-gather.15.cloned.1.call-start = ((), (), s32[]{:S(2)}) async-start(), calls=%async_computation.10 | async-start | bytes 3379200 | tf_op jit(solution)/shard_map/all_gather | solution.py:149
  10.6 372.0 %all-gather.17.cloned.1.call-start = ((), (), s32[]{:S(2)}) async-start(), calls=%async_computation.11 | async-start | bytes 3379200 | tf_op jit(solution)/shard_map/all_gather | solution.py:150
  11.1 732.8 %reduce-scatter.15.cloned.1.call-start = ((), (), s32[]{:S(2)}) async-start(), calls=%async_computation.16 | async-start | bytes 6758400 | tf_op jit(solution)/shard_map/reduce_scatter | solution.py:284
  78.2 158.9 %collective-permute-start.3 = (bf16[2,256,1280]{2,1,0:T(8,128)(2,1)}, bf16[2,256,1280]{2,1,0:T(8,128)(2,1)}, u32[]{:S(2)}, u32[]{:S(2)}) collective-permute-start(bf16[2,256,1280]{2,1,0:T(8,128)(2,1)} %bitcast.21), channel_id=1, source_target_pairs={{0,1},{1,2},{2,3},{4,5},{5,6},{6,7},{8,9},{9,10},{10,11},{12,13},{... | collective-permute-start | bytes 3932168 | tf_op jit(solution)/shard_map/ppermute | solution.py:13
  145.1 85.6 %collective-permute-start = (bf16[2,256,1280]{1,2,0:T(8,128)(2,1)}, bf16[2,256,1280]{1,2,0:T(8,128)(2,1)}, u32[]{:S(2)}, u32[]{:S(2)}) collective-permute-start(bf16[2,256,1280]{1,2,0:T(8,128)(2,1)} %bitcast.11), channel_id=1, source_target_pairs={{0,1},{1,2},{2,3},{4,5},{5,6},{6,7},{8,9},{9,10},{10,11},{12,13},{... | collective-permute-start | bytes 3932168 | tf_op jit(solution)/shard_map/ppermute | solution.py:13
  230.8 22.9 %collective-permute-start.1 = (bf16[2,256,1280]{1,2,0:T(8,128)(2,1)}, bf16[2,256,1280]{1,2,0:T(8,128)(2,1)}, u32[]{:S(2)}, u32[]{:S(2)}) collective-permute-start(bf16[2,256,1280]{1,2,0:T(8,128)(2,1)} %collective-permute-done), channel_id=1, source_target_pairs={{0,1},{1,2},{2,3},{4,5},{5,6},{6,7},{8,9},{9,10},{10,11},{12,13},{... | collective-permute-start | bytes 3932168 | tf_op jit(solution)/shard_map/ppermute | solution.py:13
  237.0 22.9 %collective-permute-start.4 = (bf16[2,256,1280]{2,1,0:T(8,128)(2,1)}, bf16[2,256,1280]{2,1,0:T(8,128)(2,1)}, u32[]{:S(2)}, u32[]{:S(2)}) collective-permute-start(bf16[2,256,1280]{2,1,0:T(8,128)(2,1)} %collective-permute-done.3), channel_id=1, source_target_pairs={{0,1},{1,2},{2,3},{4,5},{5,6},{6,7},{8,9},{9,10},{10,11},{12,13},{... | collective-permute-start | bytes 3932168 | tf_op jit(solution)/shard_map/ppermute | solution.py:13
  262.4 28.1 %collective-permute-start.5 = (bf16[2,256,1280]{2,1,0:T(8,128)(2,1)}, bf16[2,256,1280]{2,1,0:T(8,128)(2,1)}, u32[]{:S(2)}, u32[]{:S(2)}) collective-permute-start(bf16[2,256,1280]{2,1,0:T(8,128)(2,1)} %collective-permute-done.4), channel_id=1, source_target_pairs={{0,1},{1,2},{2,3},{4,5},{5,6},{6,7},{8,9},{9,10},{10,11},{12,13},{... | collective-permute-start | bytes 3932168 | tf_op jit(solution)/shard_map/ppermute | solution.py:13
  274.4 18.5 %collective-permute-start.2 = (bf16[2,256,1280]{1,2,0:T(8,128)(2,1)}, bf16[2,256,1280]{1,2,0:T(8,128)(2,1)}, u32[]{:S(2)}, u32[]{:S(2)}) collective-permute-start(bf16[2,256,1280]{1,2,0:T(8,128)(2,1)} %collective-permute-done.1), channel_id=1, source_target_pairs={{0,1},{1,2},{2,3},{4,5},{5,6},{6,7},{8,9},{9,10},{10,11},{12,13},{... | collective-permute-start | bytes 3932168 | tf_op jit(solution)/shard_map/ppermute | solution.py:13
  393.8 350.1 %reduce-scatter.13.cloned.1.call-start = ((), (), s32[]{:S(2)}) async-start(), calls=%async_computation.15 | async-start | bytes 6758400 | tf_op jit(solution)/shard_map/reduce_scatter | solution.py:283
  406.2 421.5 %reduce-scatter.17.cloned.1.call-start = ((), (), s32[]{:S(2)}) async-start(), calls=%async_computation.17 | async-start | bytes 6758400 | tf_op jit(solution)/shard_map/reduce_scatter | solution.py:285
  414.0 557.8 %reduce-scatter.9.cloned.1.call-start = ((), (), s32[]{:S(2)}) async-start(), calls=%async_computation.13 | async-start | bytes 6758400 | tf_op jit(solution)/shard_map/reduce_scatter | solution.py:281
  444.2 21.3 %collective-permute-start.6 = (bf16[2,256,1280]{1,2,0:T(8,128)(2,1)}, bf16[2,256,1280]{1,2,0:T(8,128)(2,1)}, u32[]{:S(2)}, u32[]{:S(2)}) collective-permute-start(bf16[2,256,1280]{1,2,0:T(8,128)(2,1)} %bitcast.45), channel_id=1, source_target_pairs={{1,0},{2,1},{3,2},{5,4},{6,5},{7,6},{9,8},{10,9},{11,10},{13,12},{... | collective-permute-start | bytes 3932168 | tf_op jit(solution)/shard_map/ppermute | solution.py:13
  469.0 17.2 %collective-permute-start.7 = (bf16[2,256,1280]{1,2,0:T(8,128)(2,1)}, bf16[2,256,1280]{1,2,0:T(8,128)(2,1)}, u32[]{:S(2)}, u32[]{:S(2)}) collective-permute-start(bf16[2,256,1280]{1,2,0:T(8,128)(2,1)} %fusion.19), channel_id=1, source_target_pairs={{1,0},{2,1},{3,2},{5,4},{6,5},{7,6},{9,8},{10,9},{11,10},{13,12},{... | collective-permute-start | bytes 3932168 | tf_op jit(solution)/shard_map/ppermute | solution.py:13
  488.1 31.6 %collective-permute-start.8 = (bf16[2,256,1280]{1,2,0:T(8,128)(2,1)S(1)}, bf16[2,256,1280]{1,2,0:T(8,128)(2,1)S(1)}, u32[]{:S(2)}, u32[]{:S(2)}) collective-permute-start(bf16[2,256,1280]{1,2,0:T(8,128)(2,1)S(1)} %fusion.18), channel_id=1, source_target_pairs={{1,0},{2,1},{3,2},{5,4},{6,5},{7,6},{9,8},{10,9},{11,10},{13,12},{... | collective-permute-start | bytes 3932168 | tf_op jit(solution)/shard_map/ppermute | solution.py:13
  529.0 587.0 %reduce-scatter.7.cloned.1.call-start = ((), (), s32[]{:S(2)}) async-start(), calls=%async_computation.12 | async-start | bytes 6758400 | tf_op jit(solution)/shard_map/reduce_scatter | solution.py:280
  537.6 722.4 %reduce-scatter.11.cloned.1.call-start = ((), (), s32[]{:S(2)}) async-start(), calls=%async_computation.14 | async-start | bytes 6758400 | tf_op jit(solution)/shard_map/reduce_scatter | solution.py:282
  548.0 23.6 %collective-permute-start.9 = (bf16[2,256,1280]{2,1,0:T(8,128)(2,1)}, bf16[2,256,1280]{2,1,0:T(8,128)(2,1)}, u32[]{:S(2)}, u32[]{:S(2)}) collective-permute-start(bf16[2,256,1280]{2,1,0:T(8,128)(2,1)} %copy.252), channel_id=1, source_target_pairs={{1,0},{2,1},{3,2},{5,4},{6,5},{7,6},{9,8},{10,9},{11,10},{13,12},{... | collective-permute-start | bytes 3932168 | tf_op jit(solution)/shard_map/ppermute | solution.py:13
  575.0 32.3 %collective-permute-start.10 = (bf16[2,256,1280]{2,1,0:T(8,128)(2,1)}, bf16[2,256,1280]{2,1,0:T(8,128)(2,1)}, u32[]{:S(2)}, u32[]{:S(2)}) collective-permute-start(bf16[2,256,1280]{2,1,0:T(8,128)(2,1)} %add_convert_fusion.2), channel_id=1, source_target_pairs={{1,0},{2,1},{3,2},{5,4},{6,5},{7,6},{9,8},{10,9},{11,10},{13,12},{... | collective-permute-start | bytes 3932168 | tf_op jit(solution)/shard_map/ppermute | solution.py:13
  610.8 32.4 %collective-permute-start.11 = (bf16[2,256,1280]{2,1,0:T(8,128)(2,1)}, bf16[2,256,1280]{2,1,0:T(8,128)(2,1)}, u32[]{:S(2)}, u32[]{:S(2)}) collective-permute-start(bf16[2,256,1280]{2,1,0:T(8,128)(2,1)} %add_convert_fusion.1), channel_id=1, source_target_pairs={{1,0},{2,1},{3,2},{5,4},{6,5},{7,6},{9,8},{10,9},{11,10},{13,12},{... | collective-permute-start | bytes 3932168 | tf_op jit(solution)/shard_map/ppermute | solution.py:13
  (87 other events, 1159.8 us)
Sparse Core Ops, SparseCore 0:
  10.9 61.9 all-gather.10
  75.8 58.1 all-gather.8
  136.8 58.1 all-gather.6
  197.7 58.1 all-gather.12
  258.6 61.0 all-gather.14
  322.4 60.1 all-gather.16
  393.9 144.2 reduce-scatter.14
  541.1 142.0 reduce-scatter.12
  686.1 141.4 reduce-scatter.16
  830.4 141.4 reduce-scatter.8
  974.7 141.2 reduce-scatter.6
  1118.7 141.2 reduce-scatter.10
where the time goes:
time: 1280 us; the launch traced here: 1270 us
  waiting for transfers between devices  773 us (60%)
  matrix products  195 us (15%)
  blocking collectives  113 us (9%)
  local copies, waits for them, and re-layouts  75.2 us (6%)
  other arithmetic  54.3 us (4%)
  starting transfers between devices  40.5 us (3%)
  between operations  15.8 us (1%)
    reduce_scatter x1, waiting for transfers between devices, body(): lax.psum_scatter(grad_kw, ('dp', 'seq'), scatter_dimension=0, tiled=True)  144 us
    reduce_scatter x1, waiting for transfers between devices, body(): lax.psum_scatter(grad_qw, ('dp', 'seq'), scatter_dimension=0, tiled=True)  144 us
    reduce_scatter x1, waiting for transfers between devices, body(): lax.psum_scatter(grad_vw, ('dp', 'seq'), scatter_dimension=0, tiled=True)  144 us
    unnamed x2, blocking collectives  113 us
    reduce_scatter x1, waiting for transfers between devices, body(): lax.psum_scatter(grad_downw, ('dp', 'seq'), scatter_dimension=0, tiled=True)  83.7 us
    ppermute x12, waiting for transfers between devices, shifted(): lax.ppermute(value, axis, [(source, source + steps) for source in range(i...  81.7 us
    all_gather x1, waiting for transfers between devices, body(): lax.all_gather(shards[5], ('dp', 'seq'), axis=0, tiled=True)  56.8 us
    all_gather x1, waiting for transfers between devices, body(): lax.all_gather(shards[1], ('dp', 'seq'), axis=0, tiled=True)  52.6 us
  transfers between devices with their start and end apart: 24, of which 14 were waited for; matrix products, arithmetic and copies ran while one was open for 23% of the time, Pallas kernels for 0%

commit v1 on v0

--- a/solution.py
+++ b/solution.py
@@ -1,6 +1,8 @@
 import jax
 import jax.numpy as jnp
 from jax import lax
+from jax.experimental import pallas as pl
+from jax.experimental.pallas import tpu as pltpu
 from jax.sharding import PartitionSpec as P
 
 HEADS = 16
@@ -117,6 +119,443 @@
         "shqk,sqhd->skhd", grad_scores, queries, preferred_element_type=jnp.float32
     )
     return (grad_qblock, grad_kblock, grad_vblock)
+
+
+MESH_ID = pl.DeviceIdType.MESH
+CUT = 256
+
+
+def coordinates():
+    dp = lax.axis_index("dp")
+    seq = lax.axis_index("seq")
+    return (dp // 2, lax.rem(dp, 2), seq // 2, lax.rem(seq, 2))
+
+
+def device(z, y, x, c):
+    return (z * 2 + y, x * 2 + c)
+
+
+def peers_of(z, y, x, c):
+    along = [device(lax.rem(z + k, 4), y, x, c) for k in (1, 2, 3)]
+    return along + [device(z, 1 - y, x, c), device(z, y, 1 - x, c), device(z, y, x, 1 - c)]
+
+
+def greet(peers):
+    barrier = pltpu.get_barrier_semaphore()
+    for peer in peers:
+        pl.semaphore_signal(barrier, inc=1, device_id=peer, device_id_type=MESH_ID)
+    pl.semaphore_wait(barrier, len(peers))
+
+
+def send(src, dst, sems, peer):
+    copy = pltpu.make_async_remote_copy(
+        src_ref=src,
+        dst_ref=dst,
+        send_sem=sems[0],
+        recv_sem=sems[1],
+        device_id=peer,
+        device_id_type=MESH_ID,
+    )
+    copy.start()
+    return copy
+
+
+class Gather:
+    def __init__(self, ref, cut, sems, where):
+        self.ref, self.cut, self.sems, self.where = ref, cut, sems, where
+        self.copies = [[], [], []]
+        self.phase = 0
+
+    def sem(self, i):
+        return (self.sems[0].at[i], self.sems[1].at[i])
+
+    def start(self):
+        z, y, x, c = self.where
+        ref, low, high = self.ref, pl.ds(0, self.cut), pl.ds(self.cut, self.ref.shape[-1] - self.cut)
+        phase = self.phase
+        made = []
+        if phase == 0:
+            blocks = [ref.at[z, y, x, :, low]] * 3 + [ref.at[z, y, x, :, high]]
+            for k in (1, 2, 3):
+                made.append(send(blocks[0], blocks[0], self.sem(k - 1), device(lax.rem(z + k, 4), y, x, c)))
+            made.append(send(blocks[3], blocks[3], self.sem(3), device(z, y, 1 - x, c)))
+        elif phase == 1:
+            block = ref.at[:, y, x, :, low]
+            made.append(send(block, block, self.sem(4), device(z, 1 - y, x, c)))
+            block = ref.at[z, y, :, :, high]
+            for k in (1, 2, 3):
+                made.append(send(block, block, self.sem(4 + k), device(lax.rem(z + k, 4), y, x, c)))
+        else:
+            block = ref.at[:, :, x, :, low]
+            made.append(send(block, block, self.sem(8), device(z, y, 1 - x, c)))
+            block = ref.at[:, y, :, :, high]
+            made.append(send(block, block, self.sem(9), device(z, 1 - y, x, c)))
+        self.copies[phase] = made
+        self.phase = phase + 1
+
+    def arrive(self, phase):
+        for copy in self.copies[phase]:
+            copy.wait_recv()
+
+    def sent(self):
+        for made in self.copies:
+            for copy in made:
+                copy.wait_send()
+
+
+class Scatter:
+    def __init__(self, cut, bufs, sems, where):
+        self.cut, self.bufs, self.sems, self.where = cut, bufs, sems, where
+        self.copies = []
+
+    def sem(self, i):
+        return (self.sems[0].at[i], self.sems[1].at[i])
+
+    def start(self, total):
+        z, y, x, c = self.where
+        b, cut = self.bufs, self.cut
+
+        def fill(i, _):
+            zi, yi = i // 2, lax.rem(i, 2)
+            b["sa1"][zi, yi] = total[zi, yi, 1 - x, :, :cut].astype(jnp.bfloat16)
+            b["sb1"][zi, yi] = total[zi, 1 - y, yi, :, cut:].astype(jnp.bfloat16)
+            return 0
+
+        lax.fori_loop(0, 8, fill, 0)
+        self.first = [
+            send(b["sa1"], b["ra1"], self.sem(0), device(z, y, 1 - x, c)),
+            send(b["sb1"], b["rb1"], self.sem(1), device(z, 1 - y, x, c)),
+        ]
+        self.copies += self.first
+        self.total = total
+
+    def second(self):
+        z, y, x, c = self.where
+        b, cut, total = self.bufs, self.cut, self.total
+        for copy in self.first:
+            copy.wait_recv()
+
+        def fill(zi, _):
+            b["sa2"][zi] = (total[zi, 1 - y, x, :, :cut] + b["ra1"][zi, 1 - y].astype(jnp.float32)).astype(jnp.bfloat16)
+            b["ka2"][zi] = total[zi, y, x, :, :cut] + b["ra1"][zi, y].astype(jnp.float32)
+            for xi in range(2):
+                value = total[zi, y, xi, :, cut:] + b["rb1"][zi, xi].astype(jnp.float32)
+                b["sb2"][zi, xi] = value.astype(jnp.bfloat16)
+                b["kb2"][zi, xi] = value
+            return 0
+
+        lax.fori_loop(0, 4, fill, 0)
+        self.next = [send(b["sa2"], b["ra2"], self.sem(2), device(z, 1 - y, x, c))]
+        for k in (1, 2, 3):
+            other = lax.rem(z + k, 4)
+            self.next.append(send(b["sb2"].at[other], b["rb2"].at[k - 1], self.sem(2 + k), device(other, y, x, c)))
+        self.copies += self.next
+
+    def third(self):
+        z, y, x, c = self.where
+        b = self.bufs
+        for copy in self.next:
+            copy.wait_recv()
+
+        def fill(zi, _):
+            value = b["ka2"][zi] + b["ra2"][zi].astype(jnp.float32)
+            b["ka2"][zi] = value
+            b["sa3"][zi] = value.astype(jnp.bfloat16)
+            return 0
+
+        lax.fori_loop(0, 4, fill, 0)
+
+        def value_of(xi):
+            value = b["kb2"][z, xi]
+            for k in range(3):
+                value = value + b["rb2"][k, xi].astype(jnp.float32)
+            return value
+
+        b["sb3"][...] = value_of(1 - x).astype(jnp.bfloat16)
+        b["kb3"][...] = value_of(x)
+        self.next = [send(b["sb3"], b["rb3"], self.sem(6), device(z, y, 1 - x, c))]
+        for k in (1, 2, 3):
+            other = lax.rem(z + k, 4)
+            self.next.append(send(b["sa3"].at[other], b["ra3"].at[k - 1], self.sem(6 + k), device(other, y, x, c)))
+        self.copies += self.next
+
+    def finish(self, out):
+        z, y, x, c = self.where
+        b, cut = self.bufs, self.cut
+        for copy in self.next:
+            copy.wait_recv()
+        left = b["ka2"][z]
+        for k in range(3):
+            left = left + b["ra3"][k].astype(jnp.float32)
+        right = b["kb3"][...] + b["rb3"][...].astype(jnp.float32)
+        half = left.shape[0] // 2
+        for part in range(2):
+            rows = slice(part * half, part * half + half)
+            out[part, :, :cut] = left[rows]
+            out[part, :, cut:] = right[rows]
+
+    def sent(self):
+        for copy in self.copies:
+            copy.wait_send()
+
+
+def scatter_buffers(rows, columns, cut, low):
+    wide, rest = cut, columns - cut
+    f32 = jnp.float32
+    return {
+        "sa1": pltpu.VMEM((4, 2, rows, wide), low),
+        "ra1": pltpu.VMEM((4, 2, rows, wide), low),
+        "sa2": pltpu.VMEM((4, rows, wide), low),
+        "ra2": pltpu.VMEM((4, rows, wide), low),
+        "ka2": pltpu.VMEM((4, rows, wide), f32),
+        "sa3": pltpu.VMEM((4, rows, wide), low),
+        "ra3": pltpu.VMEM((3, rows, wide), low),
+        "sb1": pltpu.VMEM((4, 2, rows, rest), low),
+        "rb1": pltpu.VMEM((4, 2, rows, rest), low),
+        "sb2": pltpu.VMEM((4, 2, rows, rest), low),
+        "rb2": pltpu.VMEM((3, 2, rows, rest), low),
+        "kb2": pltpu.VMEM((4, 2, rows, rest), f32),
+        "sb3": pltpu.VMEM((rows, rest), low),
+        "rb3": pltpu.VMEM((rows, rest), low),
+        "kb3": pltpu.VMEM((rows, rest), f32),
+    }
+
+
+def gather_kernel(*refs):
+    weights, tile = refs[:6], refs[6]
+    out, tiles = refs[7], refs[8]
+    full, own, other, ssem, rsem, gs, gr, xs, osem = refs[9:]
+    where = coordinates()
+    z, y, x, c = where
+    greet(peers_of(*where))
+    for w in range(6):
+        for h in range(2):
+            own[h, w] = weights[w][:, 640 * h : 640 * h + 640].astype(jnp.float32)
+    tiles[z, y, x, c] = tile[...]
+    sibling = device(z, y, x, 1 - c)
+    pair = send(own.at[1 - c], other, (xs.at[0], xs.at[1]), sibling)
+    pair_tile = send(tiles.at[z, y, x, c], tiles.at[z, y, x, c], (xs.at[2], xs.at[3]), sibling)
+    pair.wait_recv()
+    pair_tile.wait_recv()
+    steps = []
+    for w in range(6):
+        mine, theirs = own[c, w], other[w]
+        first = c == 0
+        block = jnp.concatenate([jnp.where(first, mine, theirs), jnp.where(first, theirs, mine)], axis=0)
+        full[w, c, z, y, x] = block.astype(jnp.bfloat16)
+        steps.append(Gather(full.at[w, c], CUT, (ssem.at[w], rsem.at[w]), where))
+    shares = []
+    stores = []
+    sends = []
+
+    def tile_step(i, block, peers):
+        made = []
+        for j, peer in enumerate(peers):
+            made.append(send(block, block, (gs.at[i + j], gr.at[i + j]), peer))
+        return made
+
+    made = tile_step(0, tiles.at[z, y, x], [device(lax.rem(z + k, 4), y, x, c) for k in (1, 2, 3)])
+    for t in range(6 + 4):
+        if t < 6:
+            steps[t].start()
+        if 0 <= t - 1 < 6:
+            steps[t - 1].arrive(0)
+            steps[t - 1].start()
+        if t == 1:
+            for m in made:
+                m.wait_recv()
+            sends += made
+            made = tile_step(3, tiles.at[:, y, x], [device(z, 1 - y, x, c)])
+        if t == 2:
+            for m in made:
+                m.wait_recv()
+            sends += made
+            made = tile_step(4, tiles.at[:, :, x], [device(z, y, 1 - x, c)])
+        if 0 <= t - 2 < 6:
+            steps[t - 2].arrive(1)
+            steps[t - 2].start()
+        if 0 <= t - 3 < 6:
+            w = t - 3
+            steps[w].arrive(2)
+            shares.append(send(full.at[w, c], full.at[w, c], (gs.at[5 + w], gr.at[5 + w]), sibling))
+        if 0 <= t - 4 < 6:
+            w = t - 4
+            shares[w].wait_recv()
+            store = pltpu.make_async_copy(full.at[w], out.at[w], osem.at[w])
+            store.start()
+            stores.append(store)
+    for m in made:
+        m.wait_recv()
+    sends += made
+    for item in steps:
+        item.sent()
+    for copy in shares + sends + [pair, pair_tile]:
+        copy.wait_send()
+    for store in stores:
+        store.wait()
+
+
+def gather_all(weights, tile):
+    dma = pltpu.SemaphoreType.DMA
+    return pl.pallas_call(
+        gather_kernel,
+        name="gather_weights",
+        out_shape=(
+            jax.ShapeDtypeStruct((6, 2, 4, 2, 2, 80, 640), jnp.bfloat16),
+            jax.ShapeDtypeStruct((4, 2, 2, 2, 8, 128), jnp.float32),
+        ),
+        in_specs=[pl.BlockSpec(memory_space=pltpu.VMEM)] * 7,
+        out_specs=(pl.BlockSpec(memory_space=pl.ANY), pl.BlockSpec(memory_space=pltpu.VMEM)),
+        scratch_shapes=[
+            pltpu.VMEM((6, 2, 4, 2, 2, 80, 640), jnp.bfloat16),
+            pltpu.VMEM((2, 6, 40, 640), jnp.float32),
+            pltpu.VMEM((6, 40, 640), jnp.float32),
+            dma((6, 10)),
+            dma((6, 10)),
+            dma((11,)),
+            dma((11,)),
+            dma((4,)),
+            dma((6,)),
+        ],
+        compiler_params=pltpu.CompilerParams(
+            collective_id=0, has_side_effects=True, vmem_limit_bytes=56 << 20
+        ),
+    )(*weights, tile)
+
+
+SEND = ("sa1", "sa2", "sa3", "sb1", "sb2", "sb3", "ka2", "kb2", "kb3")
+
+
+def scatter_kernel(*refs):
+    grads, tile = refs[:6], refs[6]
+    outs, out_tile = refs[7], refs[8]
+    big, low_send, low_recv, totals, fins, finr, lsem, ds, dr, ssem, rsem, fs, fr, tot, trecv, gs, gr = refs[9:26]
+    names = list(scatter_buffers(8, 640, CUT, jnp.bfloat16))
+    bufs = dict(zip(names, refs[26:]))
+    where = coordinates()
+    z, y, x, c = where
+    greet(peers_of(*where))
+    sibling = device(z, y, x, 1 - c)
+    loads = [
+        pltpu.make_async_copy(grads[i // 2].at[pl.ds(640 * (i % 2), 640)], big.at[i % 2], lsem.at[i])
+        for i in range(12)
+    ]
+    loads[0].start()
+    shared, fin, sends = [None] * 6, [], []
+    parts = []
+    for w in range(6):
+        mine = {k: v.at[w % 4 if k in SEND else w] for k, v in bufs.items()}
+        parts.append(Scatter(CUT, mine, (ssem.at[w], rsem.at[w]), where))
+    def tile_pass(i):
+        if i == 0:
+            return [send(tile, trecv.at[0], (gs.at[0], gr.at[0]), sibling)]
+        if i == 1:
+            tot[...] = tile[...] + trecv[0]
+            return [send(tot.at[:, :, 1 - x], trecv.at[1, :, :, 0], (gs.at[1], gr.at[1]), device(z, y, 1 - x, c))]
+        if i == 2:
+            tot[:, :, x] = tot[:, :, x] + trecv[1, :, :, 0]
+            return [send(tot.at[:, 1 - y, x], trecv.at[2, :, 0, 0], (gs.at[2], gr.at[2]), device(z, 1 - y, x, c))]
+        if i == 3:
+            tot[:, y, x] = tot[:, y, x] + trecv[2, :, 0, 0]
+            made = []
+            for k in (1, 2, 3):
+                other = lax.rem(z + k, 4)
+                made.append(send(tot.at[other, y, x], trecv.at[3, k, 0, 0], (gs.at[2 + k], gr.at[2 + k]), device(other, y, x, c)))
+            return made
+        out_tile[...] = tot[z, y, x] + trecv[3, 1, 0, 0] + trecv[3, 2, 0, 0] + trecv[3, 3, 0, 0]
+        return []
+
+    made = []
+    for t in range(6 + 5):
+        if t < 5:
+            for m in made:
+                m.wait_recv()
+            sends += made
+            made = tile_pass(t)
+        if t < 6:
+            w, slot = t, t % 2
+            if w >= 2:
+                shared[w - 2].wait_send()
+            if w >= 4:
+                parts[w - 4].sent()
+            for half in range(2):
+                i = 2 * w + half
+                if i + 1 < 12:
+                    loads[i + 1].start()
+                loads[i].wait()
+
+                def fill(j, _):
+                    rows = pl.ds(pl.multiple_of(j * 80, 80), 80)
+                    left, right = big[half, rows, :640], big[half, rows, 640:]
+                    first = c == 0
+                    totals[w % 3, half * 8 + j] = jnp.where(first, left, right)
+                    low_send[slot, half * 8 + j] = jnp.where(first, right, left).astype(jnp.bfloat16)
+                    return 0
+
+                lax.fori_loop(0, 8, fill, 0)
+            shared[w] = send(low_send.at[slot], low_recv.at[w], (ds.at[w], dr.at[w]), sibling)
+        if 0 <= t - 1 < 6:
+            w = t - 1
+            shared[w].wait_recv()
+
+            def add(i, _):
+                totals[w % 3, i] = totals[w % 3, i] + low_recv[w, i].astype(jnp.float32)
+                return 0
+
+            lax.fori_loop(0, 16, add, 0)
+            parts[w].start(totals.at[w % 3].reshape(4, 2, 2, 80, 640))
+        if 0 <= t - 2 < 6:
+            parts[t - 2].second()
+        if 0 <= t - 3 < 6:
+            parts[t - 3].third()
+        if 0 <= t - 4 < 6:
+            w = t - 4
+            parts[w].finish(fins.at[w])
+            fin.append(send(fins.at[w, 1 - c], finr.at[w], (fs.at[w], fr.at[w]), sibling))
+        if 0 <= t - 5 < 6:
+            w = t - 5
+            fin[w].wait_recv()
+            mine, theirs = fins[w, c], finr[w]
+            first = c == 0
+            outs[w, :, :640] = jnp.where(first, mine, theirs)
+            outs[w, :, 640:] = jnp.where(first, theirs, mine)
+    for part in parts[2:]:
+        part.sent()
+    for copy in shared[4:] + fin + sends:
+        copy.wait_send()
+
+
+def scatter_all(grads, tile):
+    dma = pltpu.SemaphoreType.DMA
+    low, f32 = jnp.bfloat16, jnp.float32
+    bufs = {}
+    for k, v in scatter_buffers(80, 640, CUT, low).items():
+        bufs[k] = pltpu.VMEM((4 if k in SEND else 6,) + v.shape, v.dtype)
+    return pl.pallas_call(
+        scatter_kernel,
+        name="scatter_grads",
+        out_shape=(
+            jax.ShapeDtypeStruct((6, 40, 1280), f32),
+            jax.ShapeDtypeStruct((8, 128), f32),
+        ),
+        in_specs=[pl.BlockSpec(memory_space=pl.ANY)] * 6 + [pl.BlockSpec(memory_space=pltpu.VMEM)],
+        out_specs=(pl.BlockSpec(memory_space=pltpu.VMEM), pl.BlockSpec(memory_space=pltpu.VMEM)),
+        scratch_shapes=[
+            pltpu.VMEM((2, 640, 1280), f32),
+            pltpu.VMEM((2, 16, 80, 640), low),
+            pltpu.VMEM((6, 16, 80, 640), low),
+            pltpu.VMEM((3, 16, 80, 640), f32),
+            pltpu.VMEM((6, 2, 40, 640), f32),
+            pltpu.VMEM((6, 40, 640), f32),
+            dma((12,)), dma((6,)), dma((6,)), dma((6, 10)), dma((6, 10)), dma((6,)), dma((6,)),
+            pltpu.VMEM((4, 2, 2, 8, 128), f32),
+            pltpu.VMEM((4, 4, 2, 2, 8, 128), f32),
+            dma((6,)), dma((6,)),
+        ] + list(bufs.values()),
+        compiler_params=pltpu.CompilerParams(
+            collective_id=1, has_side_effects=True, vmem_limit_bytes=60 << 20
+        ),
+    )(*grads, tile)
 
 
 def body(
@@ -300,6 +739,177 @@
     )
 
 
+def fast_body(
+    inputs,
+    w_query,
+    w_key,
+    w_value,
+    w_out,
+    w_up,
+    w_down,
+    gain_attn,
+    gain_mlp,
+    pad_patches,
+    cotangent,
+):
+    contexts, patches, model_width = inputs.shape
+    head_count = HEADS
+    head_size = HEAD_DIM
+    seq_count = lax.axis_size("seq")
+    seq_rank = lax.axis_index("seq")
+    token_rows = contexts * patches
+    shape_heads = (contexts, patches, head_count, head_size)
+    shape_flat = (contexts, patches, model_width)
+    shards = (w_query, w_key, w_value, w_out, w_up, w_down, gain_attn, gain_mlp)
+    tile = jnp.pad(jnp.stack([gain_attn, gain_mlp]).astype(jnp.float32), ((0, 6), (0, 88)))
+    gathered_w, tiles = gather_all(shards[:6], tile)
+    gathered_w = jnp.concatenate([gathered_w[:, 0], gathered_w[:, 1]], axis=-1).reshape(6, 1280, 1280)
+    gains = tiles.reshape(32, 8, 128)[:, :2, :40].swapaxes(0, 1).reshape(2, 1280)
+    gathered = tuple(gathered_w[i] for i in range(6)) + (gains[0], gains[1])
+    full_q, full_k, full_v, full_o, full_up, full_down, full_ga, full_gm = gathered
+    positions = seq_rank * patches + jnp.arange(patches, dtype=jnp.int32)
+    cosine, sine = rope_tables(positions, head_size // 2)
+    inputs_f = inputs.astype(jnp.float32).reshape(token_rows, model_width)
+    gain_one = full_ga.astype(jnp.float32)
+    scale_one = rms_scale(inputs_f)
+    flat_attn = (inputs_f * scale_one * gain_one).astype(jnp.bfloat16)
+    query_lin = jnp.dot(flat_attn, full_q, preferred_element_type=jnp.float32).reshape(shape_heads)
+    key_lin = jnp.dot(flat_attn, full_k, preferred_element_type=jnp.float32).reshape(shape_heads)
+    value_flat = jnp.dot(flat_attn, full_v, preferred_element_type=jnp.float32).astype(jnp.bfloat16)
+    queries = rotate_pairs(query_lin, cosine, sine).astype(jnp.bfloat16)
+    key_flat = rotate_pairs(key_lin, cosine, sine).astype(jnp.bfloat16)
+    own_blocks = (key_flat.reshape(shape_flat), value_flat.reshape(shape_flat))
+    kept = []
+    sources = []
+    current = own_blocks
+    for offset in range(seq_count):
+        if offset > 0:
+            current = shifted((current[0], current[1]), "seq", 1)
+        kept.append(current)
+        sources.append(seq_rank - offset)
+    stats = []
+    for block_pair, source_idx in zip(kept, sources):
+        stats.append(
+            block_forward(
+                queries,
+                block_pair[0].reshape(shape_heads),
+                block_pair[1].reshape(shape_heads),
+                source_idx,
+                positions,
+                pad_patches,
+                patches,
+            )
+        )
+    peaks = jnp.stack([entry[0] for entry in stats])
+    masses = jnp.stack([entry[1] for entry in stats])
+    partials = jnp.stack([entry[2] for entry in stats])
+    summit = jnp.max(peaks, axis=0)
+    weights_blk = jnp.exp(peaks - summit[None])
+    total = jnp.sum(weights_blk * masses, axis=0)
+    attended = (
+        jnp.sum(jnp.swapaxes(weights_blk, 2, 3)[..., None] * partials, axis=0)
+        / jnp.swapaxes(total, 1, 2)[..., None]
+    )
+    attn_low = attended.astype(jnp.bfloat16).reshape(token_rows, model_width)
+    branch = jnp.dot(attn_low, full_o, preferred_element_type=jnp.float32)
+    hidden = inputs_f + branch
+    gain_two = full_gm.astype(jnp.float32)
+    scale_two = rms_scale(hidden)
+    norm_mlp = (hidden * scale_two * gain_two).astype(jnp.bfloat16)
+    upper = jnp.dot(norm_mlp, full_up, preferred_element_type=jnp.float32)
+    active = jax.nn.silu(upper).astype(jnp.bfloat16)
+    mlp_out = jnp.dot(active, full_down, preferred_element_type=jnp.float32)
+    layer_out = (hidden + mlp_out).astype(jnp.bfloat16).reshape(shape_flat)
+    back_q, back_k, back_v, back_o, back_up, back_down, back_ga, back_gm = gathered
+    cot_low = cotangent.reshape(token_rows, model_width)
+    cot_full = cot_low.astype(jnp.float32)
+    grad_downw = jnp.dot(active.T, cot_low, preferred_element_type=jnp.float32)
+    grad_active = jnp.dot(cot_low, back_down.T, preferred_element_type=jnp.float32)
+    sigmoid_up = jax.nn.sigmoid(upper)
+    grad_upper = (grad_active * sigmoid_up * (1.0 + upper * (1.0 - sigmoid_up))).astype(
+        jnp.bfloat16
+    )
+    grad_upw = jnp.dot(norm_mlp.T, grad_upper, preferred_element_type=jnp.float32)
+    grad_norm_mlp = jnp.dot(grad_upper, back_up.T, preferred_element_type=jnp.float32)
+    grad_from_mlp, grad_gain_two = rms_back(
+        hidden, scale_two, back_gm.astype(jnp.float32), grad_norm_mlp
+    )
+    grad_hidden = cot_full + grad_from_mlp
+    hid_low = grad_hidden.astype(jnp.bfloat16)
+    grad_outw = jnp.dot(attn_low.T, hid_low, preferred_element_type=jnp.float32)
+    grad_attn = jnp.dot(hid_low, back_o.T, preferred_element_type=jnp.float32).astype(jnp.bfloat16)
+    grad_attn_f = grad_attn.astype(jnp.float32).reshape(shape_heads)
+    delta = jnp.swapaxes(jnp.sum(grad_attn_f * attended, axis=-1), 1, 2)
+    grad_queries = jnp.zeros(shape_heads, jnp.float32)
+    carried = (jnp.zeros(shape_flat, jnp.float32), jnp.zeros(shape_flat, jnp.float32))
+    for offset in reversed(range(seq_count)):
+        block_pair = kept[offset]
+        part_q, part_k, part_v = block_backward(
+            queries,
+            block_pair[0].reshape(shape_heads),
+            block_pair[1].reshape(shape_heads),
+            sources[offset],
+            positions,
+            pad_patches,
+            patches,
+            summit,
+            total,
+            delta,
+            grad_attn_f,
+        )
+        grad_queries = grad_queries + part_q
+        carried = (carried[0] + part_k.reshape(shape_flat), carried[1] + part_v.reshape(shape_flat))
+        if offset > 0:
+            carried = (
+                shifted(carried[0].astype(jnp.bfloat16), "seq", -1).astype(jnp.float32),
+                shifted(carried[1].astype(jnp.bfloat16), "seq", -1).astype(jnp.float32),
+            )
+    grad_keys, grad_values = carried
+    scale_factor = head_size ** (-0.5)
+    grad_qlin = (
+        rotate_back(grad_queries * scale_factor, cosine, sine)
+        .astype(jnp.bfloat16)
+        .reshape(token_rows, model_width)
+    )
+    grad_klin = (
+        rotate_back(grad_keys.reshape(shape_heads) * scale_factor, cosine, sine)
+        .astype(jnp.bfloat16)
+        .reshape(token_rows, model_width)
+    )
+    grad_vlin = grad_values.astype(jnp.bfloat16).reshape(token_rows, model_width)
+    grad_qw = jnp.dot(flat_attn.T, grad_qlin, preferred_element_type=jnp.float32)
+    grad_kw = jnp.dot(flat_attn.T, grad_klin, preferred_element_type=jnp.float32)
+    grad_vw = jnp.dot(flat_attn.T, grad_vlin, preferred_element_type=jnp.float32)
+    grad_norm_attn = jnp.dot(grad_qlin, back_q.T, preferred_element_type=jnp.float32)
+    grad_norm_attn = grad_norm_attn + jnp.dot(
+        grad_klin, back_k.T, preferred_element_type=jnp.float32
+    )
+    grad_norm_attn = grad_norm_attn + jnp.dot(
+        grad_vlin, back_v.T, preferred_element_type=jnp.float32
+    )
+    grad_from_attn, grad_gain_one = rms_back(
+        inputs_f, scale_one, back_ga.astype(jnp.float32), grad_norm_attn
+    )
+    grad_input = (grad_hidden + grad_from_attn).reshape(shape_flat)
+    gain_tile = jnp.stack([grad_gain_one, grad_gain_two]).reshape(2, 16, 80).swapaxes(0, 1)
+    gain_tile = jnp.pad(gain_tile, ((0, 0), (0, 6), (0, 48))).reshape(4, 2, 2, 8, 128)
+    sums, tile_sum = scatter_all((grad_qw, grad_kw, grad_vw, grad_outw, grad_upw, grad_downw), gain_tile)
+    own_gain = lax.dynamic_slice(tile_sum, (0, 40 * (seq_rank % 2)), (2, 40))
+    totals = tuple(sums[i] for i in range(6)) + (own_gain[0], own_gain[1])
+    return (
+        layer_out,
+        grad_input,
+        totals[0],
+        totals[1],
+        totals[2],
+        totals[3],
+        totals[4],
+        totals[5],
+        totals[6],
+        totals[7],
+    )
+
+
 def solution(mesh):
     placed = (
         P("dp", "seq", None),
@@ -315,7 +925,7 @@
         P("dp", "seq", None),
     )
     return jax.shard_map(
-        body,
+        fast_body if dict(mesh.shape) == {"dp": 8, "seq": 4} else body,
         mesh=mesh,
         in_specs=placed,
         out_specs=(

time: 1280 us -> 639 us (0.50)
  waiting for transfers between devices: 773 us -> 30.5 us
  Pallas kernels: 0 us -> 258 us
  blocking collectives: 113 us -> 0 us
  matrix products: 195 us -> 167 us
  between operations: 15.8 us -> 2.55 us
    reduce_scatter x6 -> x0, waiting for transfers between devices: 516 us -> none  [the longest x1 144 us: body(): lax.psum_scatter(grad_kw, ('dp', 'seq'), scatter_dimension=0, tiled=True)]
    pallas_call x0 -> x2, Pallas kernels: none -> 258 us  [the longest x1 145 us: scatter_all(): pl.pallas_call(scatter_kernel, name='scatter_grads', out_shape=(jax.Shape...]
    all_gather x6 -> x0, waiting for transfers between devices: 171 us -> none  [the longest x1 56.8 us: body(): lax.all_gather(shards[5], ('dp', 'seq'), axis=0, tiled=True)]
    unnamed x2 -> x0, blocking collectives: 113 us -> none
    ppermute x12, waiting for transfers between devices: 81.7 us -> 30.5 us  [shifted(): lax.ppermute(value, axis, [(source, source + steps) for source in range(i...]
    squeeze x0 -> x4, local copies, waits for them, and re-layouts: none -> 20.6 us  [the longest x1 8.92 us: fast_body(): gathered_w[:, 0]]
    dot_general x18, matrix products: 84.5 us -> 63.9 us  [the longest x1 6 us: fast_body(): grad_outw = jnp.dot(attn_low.T, hid_low, preferred_element_type=jnp.float32)]
    unnamed x184 -> x230, local copies, waits for them, and re-layouts: 22.9 us -> 8.21 us
  transfers between devices with their start and end apart: 24 -> 12, of which waited for: 14 -> 3; matrix products, arithmetic and copies ran while one was open for 23% -> 21% of each run, Pallas kernels for 0% -> 0%
where the time goes in v1:
time: 639 us; the launch traced here: 630 us
  Pallas kernels  258 us (40%)
  matrix products  167 us (26%)
  local copies, waits for them, and re-layouts  83.9 us (13%)
  other arithmetic  57.1 us (9%)
  waiting for transfers between devices  30.5 us (5%)
  starting transfers between devices  29.9 us (5%)
    pallas_call x1, Pallas kernels, scatter_all(): pl.pallas_call(scatter_kernel, name='scatter_grads', out_shape=(jax.Shape...  145 us
    pallas_call x1, Pallas kernels, gather_all(): pl.pallas_call(gather_kernel, name='gather_weights', out_shape=(jax.Shape...  113 us
    ppermute x12, waiting for transfers between devices, shifted(): lax.ppermute(value, axis, [(source, source + steps) for source in range(i...  30.5 us
    ppermute x12, starting transfers between devices, shifted(): lax.ppermute(value, axis, [(source, source + steps) for source in range(i...  29.9 us
    dot_general x4, matrix products, block_forward(): jnp.einsum('shqk,skhd->sqhd', expo.astype(jnp.bfloat16), value_block, pre...  27.3 us
    dot_general x4, matrix products, block_backward(): jnp.einsum('shqk,sqhd->skhd', expo.astype(jnp.bfloat16), grad_part, prefe...  22.1 us
    dot_general x4, matrix products, block_backward(): jnp.einsum('sqhd,skhd->shqk', grad_part, value_block, preferred_element_t...  17 us
    reduce_sum x4, other arithmetic, block_forward(): masses = jnp.sum(expo, axis=-1)  14.5 us
  transfers between devices with their start and end apart: 12, of which 3 were waited for; matrix products, arithmetic and copies ran while one was open for 21% of the time, Pallas kernels for 0%

profile of v1, /device:TPU:0, one launch (start us, length us, event | category | flops | bytes accessed | tf_op | source)
XLA Modules:
  0.0 629.6 jit_solution(13654586350246201456)
XLA Ops:
  1.9 113.1 %gather_weights.1 = (bf16[6,2,4,2,2,80,640]{6,5,4,3,2,1,0:T(8,128)(2,1)}, f32[4,2,2,2,8,128]{5,4,3,2,1,0:T(8,128)}) custom-call(bf16[40,1280]{1,0:T(8,128)(2,1)} %refs_0_.1, bf16[40,1280]{1,0:T(8,128)(2,1)} %refs_1_.1, bf16[40,1280]{1,0:T(8,128)(2,1)} %refs_2_.1, bf16[40,1280]{1,0:T(8,128)(2,1)} %refs_3_.1, bf16[40,1280]{1,0:T(8,128)(2,1)} %refs_4_.1, ...), custom_call_target="tpu_custom_call" | custom-call | tf_op jit(solution)/shard_map/gather_weights/pallas_call | solution.py:400
  115.0 8.7 %slice_bitcast_fusion.1 = bf16[6,4,2,2,80,640]{5,4,3,2,1,0:T(8,128)(2,1)} fusion(bf16[6,2,4,2,2,80,640]{6,5,4,3,2,1,0:T(8,128)(2,1)} %get-tuple-element.15), kind=kLoop, calls=%fused_computation.13 | loop fusion | bytes 19660800 | tf_op jit(solution)/shard_map/squeeze | solution.py:766
  123.8 8.9 %slice_bitcast_fusion = bf16[6,4,2,2,80,640]{5,4,3,2,1,0:T(8,128)(2,1)} fusion(bf16[6,2,4,2,2,80,640]{6,5,4,3,2,1,0:T(8,128)(2,1)} %get-tuple-element.15), kind=kLoop, calls=%fused_computation.12 | loop fusion | bytes 19660800 | tf_op jit(solution)/shard_map/squeeze | solution.py:766
  135.1 12.3 %fusion.5 = (bf16[1,4,2,2,80,1280]{5,4,3,2,1,0:T(8,128)(2,1)}, bf16[1,4,2,2,80,1280]{5,4,3,2,1,0:T(8,128)(2,1)}, bf16[1,4,2,2,80,1280]{5,4,3,2,1,0:T(8,128)(2,1)...) fusion(bf16[6,4,2,2,80,640]{5,4,3,2,1,0:T(8,128)(2,1)} %slice_b, ...), kind=kLoop, calls=%fused_computation.35 | loop fusion | flops 39321600 | bytes 39321600 | tf_op jit(solution)/shard_map/concatenate | solution.py:766
  154.1 5.6 copy.226
  170.8 5.6 copy.225
  191.6 5.0 reshape.787
  200.9 7.9 %convolution_bitcast_fusion.5 = f32[1,2,256,16,80]{2,4,3,1,0:T(8,128)} fusion(bf16[2,256,16,80]{1,3,2,0:T(8,128)(2,1)} %copy.228, f32[2,256,256]{1,2,0:T(8,128)} %copy-done.46, f32[2,16,256]{2,1,0:T(8,128)S(1)} %get-tuple-element.97, f32[2,16,256,256]{2,3,1,0:T(8,128)} %copy-done, pred[2,256,256]{1,2,0:T(8,128)(4,1)} %copy-done.70), kind=kOutput, calls=%fused_computation.97 | convolution fusion | flops 346030080 | bytes 13008896 | tf_op jit(solution)/shard_map/shqk,skhd->sqhd/dot_general | solution.py:82
  223.2 7.8 %convolution_bitcast_fusion.4 = f32[1,2,256,16,80]{2,4,3,1,0:T(8,128)} fusion(bf16[2,256,16,80]{1,3,2,0:T(8,128)(2,1)} %bitcast.305, f32[2,256,256]{1,2,0:T(8,128)} %get-tuple-element.28, f32[2,16,256]{2,1,0:T(8,128)S(1)} %get-tuple-element.95, f32[2,16,256,256]{2,3,1,0:T(8,128)} %copy-done.1, pred[2,256,256]{1,2,0:T(8,128)(4,1)} %get-tuple-element.29), kind=kOutput, calls=%fused_computation.96 | convolution fusion | flops 346030080 | bytes 13008896 | tf_op jit(solution)/shard_map/shqk,skhd->sqhd/dot_general | solution.py:82
  231.0 6.2 fusion.3
  239.7 5.1 collective-permute-start.5
  248.2 6.0 fusion.19
  254.3 5.3 convolution_bitcast_fusion.3
  267.1 6.4 %convolution_bitcast_fusion.2 = f32[1,2,256,16,80]{2,4,3,1,0:T(8,128)S(1)} fusion(bf16[2,256,16,80]{1,3,2,0:T(8,128)(2,1)} %bitcast.307, f32[2,256,256]{1,2,0:T(8,128)} %get-tuple-element.32, f32[2,16,256]{2,1,0:T(8,128)S(1)} %get-tuple-element.91, f32[2,16,256,256]{2,3,1,0:T(8,128)} %copy-done.37, pred[2,256,256]{1,2,0:T(8,128)(4,1)} %get-tuple-element.33), kind=kOutput, calls=%fused_computation.94 | convolution fusion | flops 346030080 | bytes 13008896 | tf_op jit(solution)/shard_map/shqk,skhd->sqhd/dot_general | solution.py:82
  302.0 5.5 reshape.788
  314.4 7.3 %fusion.45 = f32[2,16,80,256]{3,2,1,0:T(8,128)} fusion(f32[2,256,16,80]{1,3,2,0:T(8,128)S(1)} %copy.239, f32[2,256,16]{1,2,0:T(8,128)S(1)} %copy-done.96, f32[2,256,256]{1,2,0:T(8,128)S(1)} %copy-done.47, f32[2,16,256]{2,1,0:T(8,128)S(1)} %get-tuple-element.97, f32[2,16,256,256]{2,3,1,0:T(8,128)} %copy-done, pred[2,256,256]{1,2,0:T(8,128)(4,1)S(1)} %copy-done.71), kind=kOutput, calls=%fused_computation.126 | convolution fusion | flops 347340800 | bytes 14352384 | tf_op jit(solution)/shard_map/shqk,sqhd->skhd/dot_general | solution.py:108
  358.8 7.0 %convolution_convert_fusion.2 = bf16[2,16,80,256]{3,2,1,0:T(8,128)(2,1)} fusion(f32[2,256,16,80]{1,3,2,0:T(8,128)S(1)} %copy.239, f32[2,256,16]{1,2,0:T(8,128)S(1)} %copy-done.99, f32[2,256,256]{1,2,0:T(8,128)} %get-tuple-element.32, f32[2,16,256]{2,1,0:T(8,128)S(1)} %copy-done.76, f32[2,16,256,256]{2,3,1,0:T(8,128)} %copy-done.37, ...), kind=kOutput, calls=%fused_computation.98 | convolution fusion | flops 347996160 | bytes 13041664 | tf_op jit(solution)/shard_map/shqk,sqhd->skhd/dot_general | solution.py:108
  365.8 6.7 %multiply_convert_fusion.3 = bf16[2,16,256,256]{2,3,1,0:T(8,128)(2,1)} fusion(f32[2,16,256]{2,1,0:T(8,128)S(1)} %copy-done.100, bf16[2,256,16,80]{1,3,2,0:T(8,128)(2,1)S(1)} %bitcast.308, f32[2,256,256]{1,2,0:T(8,128)S(1)} %copy-done.59, f32[2,16,256]{2,1,0:T(8,128)S(1)} %copy-done.76, f32[2,16,256,256]{2,3,1,0:T(8,128)} %copy-done.37, ...), kind=kOutput, calls=%fused_computation.18 | convolution fusion | flops 351535104 | bytes 17268736 | tf_op jit(solution)/shard_map/sqhd,skhd->shqk/dot_general | solution.py:111
  391.5 6.0 fusion.40.refs_3_
  409.2 15.6 %collective-permute-done.7 = bf16[2,256,1280]{1,2,0:T(8,128)(2,1)S(1)} collective-permute-done((bf16[2,256,1280]{1,2,0:T(8,128)(2,1)S(1)}, bf16[2,256,1280]{1,2,0:T(8,128)(2,1)S(1)}, u32[]{:S(2)}, u32[]{:S(2)}) %collective-permute-start.7) | collective-permute-done | bytes 1310752 | tf_op jit(solution)/shard_map/ppermute | solution.py:15
  426.7 4.8 fusion.77.refs_5_
  437.4 10.9 %collective-permute-done.8 = bf16[2,256,1280]{1,2,0:T(8,128)(2,1)S(1)} collective-permute-done((bf16[2,256,1280]{1,2,0:T(8,128)(2,1)S(1)}, bf16[2,256,1280]{1,2,0:T(8,128)(2,1)S(1)}, u32[]{:S(2)}, u32[]{:S(2)}) %collective-permute-start.8) | collective-permute-done | bytes 1310752 | tf_op jit(solution)/shard_map/ppermute | solution.py:15
  464.5 4.9 convolution_bitcast_fusion.refs_2_
  476.1 145.3 %scatter_grads.1 = (f32[6,40,1280]{2,1,0:T(8,128)}, f32[8,128]{1,0:T(8,128)}) custom-call(f32[1280,1280]{1,0:T(8,128)} %fusion.94.refs_0_, f32[1280,1280]{1,0:T(8,128)} %fusion.95.refs_1_, f32[1280,1280]{1,0:T(8,128)} %convolution_bitcast_fusion.refs_2_, f32[1280,1280]{1,0:T(8,128)} %fusion.40.refs_3_, f32[1280,1280]{1,0:T(8,128)} %fusion.67.refs_4_, ...), custom_call_target="tpu_custom_call" | custom-call | tf_op jit(solution)/shard_map/scatter_grads/pallas_call | solution.py:534
  (352 shorter events, 209.1 us)
Async XLA Ops:
  135.1 12.3 %copy-start.64 = (bf16[2,256,1280]{2,1,0:T(8,128)(2,1)}, bf16[2,256,1280]{2,1,0:T(8,128)(2,1)S(1)}, u32[]{:S(2)}) copy-start(bf16[2,256,1280]{2,1,0:T(8,128)(2,1)S(1)} %fusion.28) | copy-start | bytes 3932164
  150.4 64.1 %collective-permute-start.3 = (bf16[2,256,1280]{2,1,0:T(8,128)(2,1)}, bf16[2,256,1280]{2,1,0:T(8,128)(2,1)}, u32[]{:S(2)}, u32[]{:S(2)}) collective-permute-start(bf16[2,256,1280]{2,1,0:T(8,128)(2,1)} %bitcast.31), channel_id=1, source_target_pairs={{0,1},{1,2},{2,3},{4,5},{5,6},{6,7},{8,9},{9,10},{10,11},{12,13},{... | collective-permute-start | bytes 3932168 | tf_op jit(solution)/shard_map/ppermute | solution.py:15
  164.2 16.5 %copy-start.77 = (f32[256,40]{0,1:T(8,128)}, f32[256,40]{0,1:T(8,128)S(1)}, u32[]{:S(2)}) copy-start(f32[256,40]{0,1:T(8,128)S(1)} %get-tuple-element.75) | copy-start | bytes 122884
  164.2 16.5 %copy-start.79 = (f32[256,40]{0,1:T(8,128)}, f32[256,40]{0,1:T(8,128)S(1)}, u32[]{:S(2)}) copy-start(f32[256,40]{0,1:T(8,128)S(1)} %get-tuple-element.76) | copy-start | bytes 122884
  166.6 42.2 %collective-permute-start = (bf16[2,256,1280]{1,2,0:T(8,128)(2,1)}, bf16[2,256,1280]{1,2,0:T(8,128)(2,1)}, u32[]{:S(2)}, u32[]{:S(2)}) collective-permute-start(bf16[2,256,1280]{1,2,0:T(8,128)(2,1)} %bitcast.19), channel_id=1, source_target_pairs={{0,1},{1,2},{2,3},{4,5},{5,6},{6,7},{8,9},{9,10},{10,11},{12,13},{... | collective-permute-start | bytes 3932168 | tf_op jit(solution)/shard_map/ppermute | solution.py:15
  200.9 10.7 %copy-start.20 = (bf16[2,256,16,40]{1,3,2,0:T(8,128)(2,1)S(1)}, bf16[2,256,16,40]{1,3,2,0:T(8,128)(2,1)}, u32[]{:S(2)}) copy-start(bf16[2,256,16,40]{1,3,2,0:T(8,128)(2,1)} %copy-done.19) | copy-start | bytes 1966084
  200.9 10.7 %copy-start.72 = (pred[2,256,256]{1,2,0:T(8,128)(4,1)S(1)}, pred[2,256,256]{1,2,0:T(8,128)(4,1)}, u32[]{:S(2)}) copy-start(pred[2,256,256]{1,2,0:T(8,128)(4,1)} %get-tuple-element.29) | copy-start | bytes 393220
  208.8 22.2 %collective-permute-start.1 = (bf16[2,256,1280]{1,2,0:T(8,128)(2,1)}, bf16[2,256,1280]{1,2,0:T(8,128)(2,1)}, u32[]{:S(2)}, u32[]{:S(2)}) collective-permute-start(bf16[2,256,1280]{1,2,0:T(8,128)(2,1)} %collective-permute-done), channel_id=1, source_target_pairs={{0,1},{1,2},{2,3},{4,5},{5,6},{6,7},{8,9},{9,10},{10,11},{12,13},{... | collective-permute-start | bytes 3932168 | tf_op jit(solution)/shard_map/ppermute | solution.py:15
  214.5 22.7 %collective-permute-start.4 = (bf16[2,256,1280]{2,1,0:T(8,128)(2,1)}, bf16[2,256,1280]{2,1,0:T(8,128)(2,1)}, u32[]{:S(2)}, u32[]{:S(2)}) collective-permute-start(bf16[2,256,1280]{2,1,0:T(8,128)(2,1)} %collective-permute-done.3), channel_id=1, source_target_pairs={{0,1},{1,2},{2,3},{4,5},{5,6},{6,7},{8,9},{9,10},{10,11},{12,13},{... | collective-permute-start | bytes 3932168 | tf_op jit(solution)/shard_map/ppermute | solution.py:15
  239.7 24.9 %collective-permute-start.5 = (bf16[2,256,1280]{2,1,0:T(8,128)(2,1)}, bf16[2,256,1280]{2,1,0:T(8,128)(2,1)}, u32[]{:S(2)}, u32[]{:S(2)}) collective-permute-start(bf16[2,256,1280]{2,1,0:T(8,128)(2,1)} %collective-permute-done.4), channel_id=1, source_target_pairs={{0,1},{1,2},{2,3},{4,5},{5,6},{6,7},{8,9},{9,10},{10,11},{12,13},{... | collective-permute-start | bytes 3932168 | tf_op jit(solution)/shard_map/ppermute | solution.py:15
  244.7 14.8 %collective-permute-start.2 = (bf16[2,256,1280]{1,2,0:T(8,128)(2,1)}, bf16[2,256,1280]{1,2,0:T(8,128)(2,1)S(1)}, u32[]{:S(2)}, u32[]{:S(2)}) collective-permute-start(bf16[2,256,1280]{1,2,0:T(8,128)(2,1)} %collective-permute-done.1), channel_id=1, source_target_pairs={{0,1},{1,2},{2,3},{4,5},{5,6},{6,7},{8,9},{9,10},{10,11},{12,13},{... | collective-permute-start | bytes 3932168 | tf_op jit(solution)/shard_map/ppermute | solution.py:15
  282.2 13.9 %copy-start.3 = (f32[512,1280]{1,0:T(8,128)}, f32[512,1280]{1,0:T(8,128)S(1)}, u32[]{:S(2)}) copy-start(f32[512,1280]{1,0:T(8,128)S(1)} %get-tuple-element.100) | copy-start | bytes 7864324
  379.8 21.1 %collective-permute-start.6 = (bf16[2,256,1280]{1,2,0:T(8,128)(2,1)}, bf16[2,256,1280]{1,2,0:T(8,128)(2,1)}, u32[]{:S(2)}, u32[]{:S(2)}) collective-permute-start(bf16[2,256,1280]{1,2,0:T(8,128)(2,1)} %bitcast.59), channel_id=1, source_target_pairs={{1,0},{2,1},{3,2},{5,4},{6,5},{7,6},{9,8},{10,9},{11,10},{13,12},{... | collective-permute-start | bytes 3932168 | tf_op jit(solution)/shard_map/ppermute | solution.py:15
  381.1 24.9 %collective-permute-start.9 = (bf16[2,256,1280]{2,1,0:T(8,128)(2,1)}, bf16[2,256,1280]{2,1,0:T(8,128)(2,1)}, u32[]{:S(2)}, u32[]{:S(2)}) collective-permute-start(bf16[2,256,1280]{2,1,0:T(8,128)(2,1)} %copy.262), channel_id=1, source_target_pairs={{1,0},{2,1},{3,2},{5,4},{6,5},{7,6},{9,8},{10,9},{11,10},{13,12},{... | collective-permute-start | bytes 3932168 | tf_op jit(solution)/shard_map/ppermute | solution.py:15
  403.5 21.3 %collective-permute-start.7 = (bf16[2,256,1280]{1,2,0:T(8,128)(2,1)S(1)}, bf16[2,256,1280]{1,2,0:T(8,128)(2,1)S(1)}, u32[]{:S(2)}, u32[]{:S(2)}) collective-permute-start(bf16[2,256,1280]{1,2,0:T(8,128)(2,1)S(1)} %fusion.25), channel_id=1, source_target_pairs={{1,0},{2,1},{3,2},{5,4},{6,5},{7,6},{9,8},{10,9},{11,10},{13,12},{... | collective-permute-start | bytes 3932168 | tf_op jit(solution)/shard_map/ppermute | solution.py:15
  406.0 18.8 %copy-start.30 = (f32[2,16,80,256]{3,2,1,0:T(8,128)S(1)}, f32[2,16,80,256]{3,2,1,0:T(8,128)}, u32[]{:S(2)}) copy-start(f32[2,16,80,256]{3,2,1,0:T(8,128)} %fusion.79) | copy-start | bytes 7864324
  407.7 19.0 %copy-start.67 = (bf16[2,256,1280]{2,1,0:T(8,128)(2,1)S(1)}, bf16[2,256,1280]{2,1,0:T(8,128)(2,1)}, u32[]{:S(2)}) copy-start(bf16[2,256,1280]{2,1,0:T(8,128)(2,1)} %param.21) | copy-start | bytes 3932164
  407.7 27.7 %collective-permute-start.10 = (bf16[2,256,1280]{2,1,0:T(8,128)(2,1)S(1)}, bf16[2,256,1280]{2,1,0:T(8,128)(2,1)S(1)}, u32[]{:S(2)}, u32[]{:S(2)}) collective-permute-start(bf16[2,256,1280]{2,1,0:T(8,128)(2,1)S(1)} %add_convert_fusion.2), channel_id=1, source_target_pairs={{1,0},{2,1},{3,2},{5,4},{6,5},{7,6},{9,8},{10,9},{11,10},{13,12},{... | collective-permute-start | bytes 3932168 | tf_op jit(solution)/shard_map/ppermute | solution.py:15
  425.1 23.1 %collective-permute-start.8 = (bf16[2,256,1280]{1,2,0:T(8,128)(2,1)S(1)}, bf16[2,256,1280]{1,2,0:T(8,128)(2,1)S(1)}, u32[]{:S(2)}, u32[]{:S(2)}) collective-permute-start(bf16[2,256,1280]{1,2,0:T(8,128)(2,1)S(1)} %fusion.24), channel_id=1, source_target_pairs={{1,0},{2,1},{3,2},{5,4},{6,5},{7,6},{9,8},{10,9},{11,10},{13,12},{... | collective-permute-start | bytes 3932168 | tf_op jit(solution)/shard_map/ppermute | solution.py:15
  431.4 16.8 %copy-start.27 = (f32[2,16,80,256]{3,2,1,0:T(8,128)S(1)}, f32[2,16,80,256]{3,2,1,0:T(8,128)}, u32[]{:S(2)}) copy-start(f32[2,16,80,256]{3,2,1,0:T(8,128)} %fusion.78) | copy-start | bytes 7864324
  435.7 12.9 %copy-start.78 = (f32[256,40]{0,1:T(8,128)S(1)}, f32[256,40]{0,1:T(8,128)}, u32[]{:S(2)}) copy-start(f32[256,40]{0,1:T(8,128)} %copy-done.77) | copy-start | bytes 122884
  435.7 12.9 %copy-start.80 = (f32[256,40]{0,1:T(8,128)S(1)}, f32[256,40]{0,1:T(8,128)}, u32[]{:S(2)}) copy-start(f32[256,40]{0,1:T(8,128)} %copy-done.79) | copy-start | bytes 122884
  435.7 28.4 %collective-permute-start.11 = (bf16[2,256,1280]{2,1,0:T(8,128)(2,1)S(1)}, bf16[2,256,1280]{2,1,0:T(8,128)(2,1)S(1)}, u32[]{:S(2)}, u32[]{:S(2)}) collective-permute-start(bf16[2,256,1280]{2,1,0:T(8,128)(2,1)S(1)} %add_convert_fusion.1), channel_id=1, source_target_pairs={{1,0},{2,1},{3,2},{5,4},{6,5},{7,6},{9,8},{10,9},{11,10},{13,12},{... | collective-permute-start | bytes 3932168 | tf_op jit(solution)/shard_map/ppermute | solution.py:15
  476.1 149.1 %copy-start.103 = (f32[512]{0:T(512)S(1)}, f32[512]{0:T(512)}, u32[]{:S(2)}) copy-start(f32[512]{0:T(512)} %multiply_multiply_fusion) | copy-start | bytes 6148
  (101 other events, 437.5 us)
